TPU v7x, 32 devices: a whole 2x2x4 slice. The times are simulated.
32 devices in a mesh: query: 2 (over x), gallery: 16 (over z, y, core).
Axes of the slice: x: 2, y: 2, z: 4, core: 2. Of those that a mesh axis runs over, the one named last changes fastest.
Arguments:
- query_hidden: bfloat16 [768, 32, 768], P(('query', 'gallery')), may hold values from -6 to 6
- query_mask: int32 [768, 32], P(('query', 'gallery')), may hold values 0 or 1
- passage_hidden: bfloat16 [16, 360, 768], P('gallery', 'query'), may hold values from -6 to 6
- passage_ids: int32 [16, 360], P('gallery', 'query'), may hold values from 999 to 30521, as said below
- passage_lengths: int32 [32], P('gallery'), may hold values from 30 to 180, as said below
- projection: bfloat16 [768, 128], replicated, may hold values from -0.21875 to 0.21875
Outputs:
- scores: float32 [768, 32], P(('query', 'gallery'))
Inputs may be any that keep to these rules, and one draw needn't show every extreme that they name: `passage_ids`: ids from 999 to 1066 are punctuation; the rest are words. `passage_lengths`: some passage has exactly 180 tokens.
All inputs are finite; a program needn't handle non-finite values. No bound on the sum of `query_mask` on one device may be relied on, other than what follows from the above.
Results may differ from a plain program's by a relative error of at most 0.00036.
Values may be sent and summed in bfloat16 or wider, within the bound.
A program may use at most 64 MiB of HBM per device.

v0:
```python
import math

import jax
import jax.numpy as jnp
from jax import lax
from jax.sharding import PartitionSpec as P

DIM = 128
PLEN = 180
QLEN = 32
PUNCT_LO = 999
PUNCT_HI = 1067
PASS_GRP = 2


EPS = 1e-06
NEG = -1000000000.0


def unit_rows(hidden, projection):
    flat_rows = hidden.reshape(-1, hidden.shape[-1])
    projected = jnp.dot(flat_rows, projection, preferred_element_type=jnp.float32)
    inverse_norm = lax.rsqrt(jnp.sum(projected * projected, axis=-1, keepdims=True) + EPS)
    return (projected * inverse_norm).astype(jnp.bfloat16)


def local(query_hidden, query_mask, passage_hidden, passage_ids, passage_lengths, projection):
    row_count = passage_hidden.shape[1]
    query_count = query_hidden.shape[0]
    groups = lax.axis_size("gallery")
    query_block = lax.axis_index("query")
    position = query_block * row_count + jnp.arange(row_count, dtype=jnp.int32)
    passage_slot = position // PLEN
    token_pos = position % PLEN
    onehot = passage_slot[:, None] == jnp.arange(PASS_GRP, dtype=jnp.int32)[None, :]
    length_rows = jnp.sum(jnp.where(onehot, passage_lengths[None, :], 0), axis=1)
    token_ids = passage_ids[0]
    punctuation = (token_ids >= PUNCT_LO) & (token_ids < PUNCT_HI)
    kept = (token_pos < length_rows) & ((token_pos == 0) | jnp.logical_not(punctuation))
    kept_flag = kept.astype(jnp.bfloat16)[None, :]
    passage_unit = unit_rows(passage_hidden, projection).reshape(1, row_count, DIM)
    query_unit = unit_rows(query_hidden, projection)
    weights = query_mask.astype(jnp.float32).reshape(-1)
    thin_units, thin_flags = (
        lax.all_gather(passage_unit, "gallery", axis=0, tiled=True),
        lax.all_gather(kept_flag, "gallery", axis=0, tiled=True),
    )
    initial = jnp.full((query_unit.shape[0], groups * PASS_GRP), NEG, jnp.float32)
    piece_units = lax.all_gather(thin_units, "query", axis=1, tiled=True)
    piece_flags = lax.all_gather(thin_flags, "query", axis=1, tiled=True)
    piece_rows = piece_units.shape[1]
    row_slot = jnp.arange(piece_rows, dtype=jnp.int32) // PLEN
    block_width = math.gcd(groups, 4)
    unit_blocks = piece_units.reshape(groups // block_width, block_width * piece_rows, DIM)
    flag_blocks = piece_flags.reshape(groups // block_width, 1, block_width * piece_rows)

    def one_block(block_pair):
        unit_block, flag_block = block_pair
        similar = jnp.einsum(
            "td,rd->tr", query_unit, unit_block, preferred_element_type=jnp.float32
        )
        similar = jnp.where(flag_block > 0, similar, NEG).reshape(-1, block_width, piece_rows)
        per_member = [
            jnp.max(jnp.where(row_slot == member, similar, NEG), axis=2)
            for member in range(PASS_GRP)
        ]
        return jnp.stack(per_member, axis=2)

    fresh_max = lax.map(one_block, (unit_blocks, flag_blocks))
    fresh_max = jnp.transpose(fresh_max, (1, 0, 2, 3)).reshape(initial.shape)
    running = jnp.maximum(initial, fresh_max)
    scores = jnp.sum(
        (running * weights[:, None]).reshape(query_count, QLEN, groups * PASS_GRP), axis=1
    )
    return scores


def solution(mesh):
    placed = (
        P(("query", "gallery"), None, None),
        P(("query", "gallery"), None),
        P("gallery", "query", None),
        P("gallery", "query"),
        P("gallery"),
        P(),
    )
    return jax.shard_map(
        local, mesh=mesh, in_specs=placed, out_specs=P(("query", "gallery"), None), check_vma=False
    )
```

profile of v0, /device:TPU:0, one launch (start us, length us, event | category | flops | bytes accessed | tf_op | source)
XLA Modules:
  0.0 77.6 jit_solution(7608371529911874838)
XLA Ops:
  6.5 0.0 copy-start
  6.5 0.0 all-gather.6.cloned.1.call-start
  6.5 1.4 %multiply_reduce_fusion.2 = (f32[180]{0:T(256)S(1)}, f32[180,128]{1,0:T(8,128)S(1)}) fusion(bf16[768,128]{1,0:T(8,128)(2,1)} %param.13, bf16[1,180,768]{2,1,0:T(8,128)(2,1)} %param.10), kind=kOutput, calls=%fused_computation.26 | convolution fusion | flops 35435340 | bytes 565968 | tf_op jit(solution)/shard_map/dot_general | solution.py:22
  8.0 0.1 fusion.11
  8.1 0.0 copy-start.1
  8.1 25.5 %all-gather.3 = bf16[16,180,128]{2,1,0:T(8,128)(2,1)S(1)} all-gather(bf16[1,180,128]{2,1,0:T(8,128)(2,1)S(1)} %fusion.11), channel_id=2, replica_groups=mesh['query'=2,'gallery'=16] {'gallery'}, dimensions={0}, use_global_device_ids=true | all-gather | bytes 783360 | tf_op jit(solution)/shard_map/all_gather | solution.py:45
  33.6 1.0 %copy.25 = bf16[16,180,128]{2,0,1:T(8,128)(2,1)} copy(bf16[16,180,128]{2,1,0:T(8,128)(2,1)S(1)} %all-gather.3) | data formatting | bytes 1474560 | tf_op jit(solution)/shard_map/all_gather | solution.py:45
  34.6 0.0 all-gather.6.cloned.1.call-update
  34.6 0.0 copy-start.4
  34.6 0.0 copy-start.3
  34.7 0.0 copy-done
  34.7 0.0 copy-done.1
  34.7 0.0 copy-start.2
  34.7 0.6 multiply_reduce_fusion.1
  35.3 0.2 copy.28
  35.5 0.0 copy-done.4
  35.5 0.1 fusion.12
  35.6 0.0 copy-done.3
  35.6 17.5 %all-gather.1 = bf16[16,1,180]{2,1,0:T(2,128)(2,1)S(1)} all-gather(bf16[1,1,180]{2,1,0:T(2,128)(2,1)S(1)} %fusion.13), channel_id=1, replica_groups=mesh['query'=2,'gallery'=16] {'gallery'}, dimensions={0}, use_global_device_ids=true | all-gather | bytes 6120 | tf_op jit(solution)/shard_map/all_gather | solution.py:46
  53.1 4.5 %all-gather.2 = bf16[2,180,16]{1,2,0:T(8,128)(2,1)S(1)} all-gather(bf16[1,180,16]{1,2,0:T(8,128)(2,1)S(1)} %bitcast.56), channel_id=1, replica_groups=mesh['query'=2,'gallery'=16] {'query'}, dimensions={0}, use_global_device_ids=true | all-gather | bytes 17280 | tf_op jit(solution)/shard_map/all_gather | solution.py:50
  57.6 0.1 reshape.108
  57.7 0.1 reshape.113
  57.8 0.0 copy-done.2
  57.8 0.5 all-gather.6.cloned.1.call-done
  58.3 1.8 %copy.26 = bf16[16,360,128]{2,1,0:T(8,128)(2,1)S(1)} copy(bf16[16,360,128]{2,0,1:T(8,128)(2,1)} %all-gather.6.cloned.1.call-done) | data formatting | bytes 2949120 | tf_op jit(solution)/shard_map/all_gather | solution.py:49
  60.1 9.6 %while.12 = (s32[]{:T(128)}, f32[4,768,4,2]{1,3,2,0:T(2,128)S(1)}, bf16[4,1,1440]{2,1,0:T(2,128)(2,1)S(1)}, bf16[4,1440,128]{2,1,0:T(8,128)(2,1)S(1)}, bf16[768,128]{1,0:T(8,128)(2,1)S(1)}, /*index=5*/s32[]{:T(128)}) while((s32[]{:T(128)}, f32[4,768,4,2]{1,3,2,0:T(2,128)S(1)}, bf16[4,1,1440]{2,1,0:T(2,128)(2,1)S(1)}, ...), condition=%wide.region_6.7_spmd.clone.clone, body=%wide.region_3.6_spmd.clone.clone.sunk | while | flops 288650176 | bytes 9543377 | solution.py:69
  60.2 1.1 %convolution_select_fusion.2 = f32[1440,768]{1,0:T(8,128)S(1)} fusion(bf16[768,128]{1,0:T(8,128)(2,1)S(1)} %get-tuple-element.172, pred[1440]{0:T(1024)(128)(4,1)S(1)} %compare_reduce_fusion.2, bf16[4,1440,128]{2,1,0:T(8,128)(2,1)S(1)} %get-tuple-element.171, s32[]{:T(128)} %get-tuple-element.162), kind=kOutput, calls=%fused_computation.3.clone.1 | convolution fusion | flops 284221440 | bytes 4990980 | tf_op jit(solution)/shard_map/while/body/eval_jaxpr/td,rd->tr/dot_general | solution.py:59
  61.3 1.1 %select_reduce_fusion.3 = (f32[768,4]{0,1:T(4,128)S(1)}, f32[768,4]{0,1:T(4,128)S(1)}) fusion(f32[768,4,360]{0,2,1:T(8,128)S(1)} %bitcast.53, pred[360]{0:T(512)(128)(4,1)S(1)} %get-tuple-element.152, pred[360]{0:T(512)(128)(4,1)S(1)} %get-tuple-element.153), kind=kLoop, calls=%fused_computation.2.clone.1 | loop fusion | flops 4417536 | bytes 4448976 | tf_op jit(solution)/shard_map/while/body/eval_jaxpr/reduce_max | solution.py:64
  62.5 1.1 %convolution_select_fusion.2 = f32[1440,768]{1,0:T(8,128)S(1)} fusion(bf16[768,128]{1,0:T(8,128)(2,1)S(1)} %get-tuple-element.172, pred[1440]{0:T(1024)(128)(4,1)S(1)} %compare_reduce_fusion.2, bf16[4,1440,128]{2,1,0:T(8,128)(2,1)S(1)} %get-tuple-element.171, s32[]{:T(128)} %get-tuple-element.162), kind=kOutput, calls=%fused_computation.3.clone.1 | convolution fusion | flops 284221440 | bytes 4990980 | tf_op jit(solution)/shard_map/while/body/eval_jaxpr/td,rd->tr/dot_general | solution.py:59
  63.7 1.1 %select_reduce_fusion.3 = (f32[768,4]{0,1:T(4,128)S(1)}, f32[768,4]{0,1:T(4,128)S(1)}) fusion(f32[768,4,360]{0,2,1:T(8,128)S(1)} %bitcast.53, pred[360]{0:T(512)(128)(4,1)S(1)} %get-tuple-element.152, pred[360]{0:T(512)(128)(4,1)S(1)} %get-tuple-element.153), kind=kLoop, calls=%fused_computation.2.clone.1 | loop fusion | flops 4417536 | bytes 4448976 | tf_op jit(solution)/shard_map/while/body/eval_jaxpr/reduce_max | solution.py:64
  64.9 1.1 %convolution_select_fusion.2 = f32[1440,768]{1,0:T(8,128)S(1)} fusion(bf16[768,128]{1,0:T(8,128)(2,1)S(1)} %get-tuple-element.172, pred[1440]{0:T(1024)(128)(4,1)S(1)} %compare_reduce_fusion.2, bf16[4,1440,128]{2,1,0:T(8,128)(2,1)S(1)} %get-tuple-element.171, s32[]{:T(128)} %get-tuple-element.162), kind=kOutput, calls=%fused_computation.3.clone.1 | convolution fusion | flops 284221440 | bytes 4990980 | tf_op jit(solution)/shard_map/while/body/eval_jaxpr/td,rd->tr/dot_general | solution.py:59
  66.1 1.1 %select_reduce_fusion.3 = (f32[768,4]{0,1:T(4,128)S(1)}, f32[768,4]{0,1:T(4,128)S(1)}) fusion(f32[768,4,360]{0,2,1:T(8,128)S(1)} %bitcast.53, pred[360]{0:T(512)(128)(4,1)S(1)} %get-tuple-element.152, pred[360]{0:T(512)(128)(4,1)S(1)} %get-tuple-element.153), kind=kLoop, calls=%fused_computation.2.clone.1 | loop fusion | flops 4417536 | bytes 4448976 | tf_op jit(solution)/shard_map/while/body/eval_jaxpr/reduce_max | solution.py:64
  67.3 1.1 %convolution_select_fusion.2 = f32[1440,768]{1,0:T(8,128)S(1)} fusion(bf16[768,128]{1,0:T(8,128)(2,1)S(1)} %get-tuple-element.172, pred[1440]{0:T(1024)(128)(4,1)S(1)} %compare_reduce_fusion.2, bf16[4,1440,128]{2,1,0:T(8,128)(2,1)S(1)} %get-tuple-element.171, s32[]{:T(128)} %get-tuple-element.162), kind=kOutput, calls=%fused_computation.3.clone.1 | convolution fusion | flops 284221440 | bytes 4990980 | tf_op jit(solution)/shard_map/while/body/eval_jaxpr/td,rd->tr/dot_general | solution.py:59
  68.5 1.1 %select_reduce_fusion.3 = (f32[768,4]{0,1:T(4,128)S(1)}, f32[768,4]{0,1:T(4,128)S(1)}) fusion(f32[768,4,360]{0,2,1:T(8,128)S(1)} %bitcast.53, pred[360]{0:T(512)(128)(4,1)S(1)} %get-tuple-element.152, pred[360]{0:T(512)(128)(4,1)S(1)} %get-tuple-element.153), kind=kLoop, calls=%fused_computation.2.clone.1 | loop fusion | flops 4417536 | bytes 4448976 | tf_op jit(solution)/shard_map/while/body/eval_jaxpr/reduce_max | solution.py:64
  69.7 0.1 maximum_bitcast_fusion.1
  69.7 0.2 max_broadcast_in_dim.12
  69.9 0.2 multiply_reduce_fusion
  70.1 0.7 copy.29
  (29 shorter events, 0.6 us)
Async XLA Ops:
  6.5 28.1 %copy-start = (bf16[24,32,768]{2,1,0:T(8,128)(2,1)S(1)}, bf16[24,32,768]{2,1,0:T(8,128)(2,1)}, u32[]{:S(2)}) copy-start(bf16[24,32,768]{2,1,0:T(8,128)(2,1)} %param.8) | copy-start | bytes 3538948
  6.5 51.8 %all-gather.6.cloned.1.call-start = ((), (), s32[]{:S(2)}) async-start(), calls=%async_computation | async-start | bytes 2211840 | tf_op jit(solution)/shard_map/all_gather | solution.py:49
  8.1 26.6 %copy-start.1 = (bf16[768,128]{1,0:T(8,128)(2,1)S(1)}, bf16[768,128]{1,0:T(8,128)(2,1)}, u32[]{:S(2)}) copy-start(bf16[768,128]{1,0:T(8,128)(2,1)} %param.13) | copy-start | bytes 589828
  34.6 0.9 %copy-start.4 = (s32[2]{0:T(128)S(1)}, s32[2]{0:T(128)}, u32[]{:S(2)}) copy-start(s32[2]{0:T(128)} %param.12) | copy-start | bytes 28
  34.6 1.0 %copy-start.3 = (s32[1,180]{1,0:T(1,128)S(1)}, s32[1,180]{1,0:T(1,128)}, u32[]{:S(2)}) copy-start(s32[1,180]{1,0:T(1,128)} %param.11) | copy-start | bytes 2164
  34.7 23.1 %copy-start.2 = (s32[24,32]{1,0:T(8,128)S(1)}, s32[24,32]{1,0:T(8,128)}, u32[]{:S(2)}) copy-start(s32[24,32]{1,0:T(8,128)} %param.9) | copy-start | bytes 9220
Sparse Core Ops, SparseCore 0:
  34.7 23.5 all-gather.5
where the time goes:
time: 77.8 us; the launch traced here: 77.6 us
  blocking collectives  47.5 us (61%)
  between operations  13.6 us (17%)
  matrix products  6.51 us (8%)
  other arithmetic  5.26 us (7%)
  local copies, waits for them, and re-layouts  4.07 us (5%)
    all_gather x1, blocking collectives, local(): lax.all_gather(passage_unit, 'gallery', axis=0, tiled=True)  25.5 us
    all_gather x1, blocking collectives, local(): lax.all_gather(kept_flag, 'gallery', axis=0, tiled=True)  17.5 us
    dot_general x4, matrix products, one_block(): jnp.einsum('td,rd->tr', query_unit, unit_block, preferred_element_type=jn...  4.52 us
    all_gather x1, blocking collectives, local(): piece_flags = lax.all_gather(thin_flags, 'query', axis=1, tiled=True)  4.49 us
    reduce_max x4, other arithmetic, one_block(): jnp.max(jnp.where(row_slot == member, similar, NEG), axis=2)  4.39 us
    dot_general x2, matrix products, unit_rows(): jnp.dot(flat_rows, projection, preferred_element_type=jnp.float32)  2 us
    all_gather x1, local copies, waits for them, and re-layouts, local(): piece_units = lax.all_gather(thin_units, 'query', axis=1, tiled=True)  1.75 us
  transfers between devices with their start and end apart: 1, of which 1 were waited for; matrix products, arithmetic and copies ran while one was open for 1% of the time, Pallas kernels for 0%

commit v1 on v0

--- a/solution.py
+++ b/solution.py
@@ -3,6 +3,8 @@
 import jax
 import jax.numpy as jnp
 from jax import lax
+from jax.experimental import pallas as pl
+from jax.experimental.pallas import tpu as pltpu
 from jax.sharding import PartitionSpec as P
 
 DIM = 128
@@ -75,6 +77,219 @@
     return scores
 
 
+ROWS = 192
+HALF = 96
+MESH = pl.DeviceIdType.MESH
+
+
+def fused_kernel(
+    qh_hbm, mask_hbm, ph_hbm, ids_hbm, len_hbm, proj_hbm, out_ref,
+    qh, mask, ph, ids, lens, proj, padded, blocks, queries, best, part_out, part_in,
+    in_sem, z_send, z_recv, n_send, n_recv, c_send, c_recv,
+):
+    x = lax.axis_index("query")
+    g = lax.axis_index("gallery")
+    core = g % 2
+    y = (g // 2) % 2
+    z = g // 4
+    rows = ph.shape[0]
+    qcount, qlen = mask.shape
+    width = qcount * qlen
+
+    def at(zz, yy, cc):
+        return (zz * 2 + yy) * 2 + cc
+
+    line = [(x, at((z + 4 - d) % 4, y, core)) for d in range(4)]
+    x_near = (1 - x, g)
+    y_near = (x, at(z, 1 - y, core))
+    twin = (x, at(z, y, 1 - core))
+
+    barrier = pltpu.get_barrier_semaphore()
+    for peer in (line[1], line[2], line[3], x_near, y_near, twin):
+        pl.semaphore_signal(barrier, inc=1, device_id=peer, device_id_type=MESH)
+
+    loads = [
+        pltpu.make_async_copy(src, dst, in_sem.at[k])
+        for k, (src, dst) in enumerate(
+            [(ph_hbm.at[0], ph), (proj_hbm, proj), (ids_hbm, ids), (len_hbm, lens), (mask_hbm, mask), (qh_hbm, qh)]
+        )
+    ]
+    for load in loads:
+        load.start()
+    best[...] = jnp.zeros(best.shape, jnp.float32)
+
+    for load in loads[:4]:
+        load.wait()
+    projected = jnp.dot(ph[...], proj[...], preferred_element_type=jnp.float32)
+    unit = projected * lax.rsqrt(jnp.sum(projected * projected, axis=-1, keepdims=True) + EPS)
+    tokens = ids[...]
+    slot = lax.broadcasted_iota(jnp.int32, tokens.shape, 1)
+    punctuation = (tokens >= PUNCT_LO) & (tokens < PUNCT_HI)
+    kept = (slot < lens[x]) & ((slot == 0) | jnp.logical_not(punctuation))
+    kept = jnp.where(kept, 1.0, 0.0)
+    eye = lax.broadcasted_iota(jnp.int32, (rows, rows), 0) == lax.broadcasted_iota(jnp.int32, (rows, rows), 1)
+    column = jnp.sum(jnp.where(eye, jnp.broadcast_to(kept, (rows, rows)), 0.0), axis=1, keepdims=True)
+    first = unit[0:1, :]
+    padded[...] = jnp.broadcast_to(first, padded.shape)
+    padded[pl.ds(0, rows), :] = jnp.where(column > 0.0, unit, first)
+    blocks[0] = padded[...].astype(jnp.bfloat16)
+
+    pl.semaphore_wait(barrier, 6)
+
+    def remote(src, dst, send, recv, peer):
+        return pltpu.make_async_remote_copy(
+            src_ref=src, dst_ref=dst, send_sem=send, recv_sem=recv, device_id=peer, device_id_type=MESH
+        )
+
+    along_z = {
+        d: remote(blocks.at[0], blocks.at[4 * d], z_send.at[d], z_recv.at[d], line[d]) for d in (1, 2, 3)
+    }
+
+    def near(d, kind):
+        if kind == 0:
+            pair, peer = (blocks.at[4 * d], blocks.at[4 * d + 2]), x_near
+        elif kind == 1:
+            pair, peer = (blocks.at[4 * d], blocks.at[4 * d + 1]), y_near
+        elif kind == 2:
+            half = pl.ds(0, HALF)
+            pair, peer = (blocks.at[4 * d + 2, half], blocks.at[4 * d + 3, half]), y_near
+        else:
+            half = pl.ds(HALF, HALF)
+            pair, peer = (blocks.at[4 * d + 1, half], blocks.at[4 * d + 3, half]), x_near
+        k = 4 * d + kind
+        return remote(*pair, n_send.at[k], n_recv.at[k], peer)
+
+    side = {(d, kind): near(d, kind) for d in range(4) for kind in range(4)}
+
+    def score(d, dx, dy):
+        passage = ((((z + d) % 4) * 2 + (y + dy) % 2) * 2 + core) * 2 + (x + dx) % 2
+        held = 4 * d + 2 * dx + dy
+
+        def chunk(k, carry):
+            cols = pl.ds(pl.multiple_of(k * 256, 256), 256)
+            similar = jnp.dot(blocks[held], queries[:, cols], preferred_element_type=jnp.float32)
+            best[pl.ds(passage, 1), cols] = jnp.max(similar, axis=0, keepdims=True)
+            return carry
+
+        lax.fori_loop(0, 2 * width // 256, chunk, 0)
+
+    side[0, 0].start()
+    side[0, 1].start()
+    along_z[1].start()
+    along_z[3].start()
+    along_z[2].start()
+
+    loads[4].wait()
+    flags = mask[...].astype(jnp.float32)
+    spread = lax.broadcasted_iota(jnp.int32, (qlen, width), 1) % qlen == lax.broadcasted_iota(jnp.int32, (qlen, width), 0)
+    spread = jnp.dot(flags, jnp.where(spread, 1.0, 0.0), preferred_element_type=jnp.float32)
+    member = lax.broadcasted_iota(jnp.int32, (qcount, width), 1) // qlen == lax.broadcasted_iota(jnp.int32, (qcount, width), 0)
+    weight = jnp.sum(jnp.where(member, spread, 0.0), axis=0, keepdims=True)
+    loads[5].wait()
+    for k in range(width // 256):
+        cols = slice(k * 256, (k + 1) * 256)
+        projected = jnp.dot(qh[cols, :], proj[...], preferred_element_type=jnp.float32).T
+        unit = projected * lax.rsqrt(jnp.sum(projected * projected, axis=0, keepdims=True) + EPS)
+        queries[:, cols] = (unit * weight[:, cols]).astype(jnp.bfloat16)
+    own, other = pl.ds(0, width), pl.ds(width, width)
+    swap = remote(queries.at[:, own], queries.at[:, other], c_send.at[0], c_recv.at[0], twin)
+    swap.start()
+
+    def pass_on(d):
+        side[d, 0].wait_recv()
+        side[d, 2].start()
+        side[d, 1].wait_recv()
+        side[d, 3].start()
+
+    def corner(d):
+        side[d, 2].wait_recv()
+        side[d, 3].wait_recv()
+        score(d, 1, 1)
+
+    def from_line(d):
+        along_z[d].wait_recv()
+        side[d, 0].start()
+        side[d, 1].start()
+
+    pass_on(0)
+    from_line(1)
+    from_line(3)
+    swap.wait_recv()
+    score(0, 0, 0)
+    score(0, 1, 0)
+    score(0, 0, 1)
+    from_line(2)
+    score(1, 0, 0)
+    score(3, 0, 0)
+    corner(0)
+    pass_on(1)
+    score(1, 1, 0)
+    score(1, 0, 1)
+    pass_on(3)
+    score(3, 1, 0)
+    score(3, 0, 1)
+    score(2, 0, 0)
+    pass_on(2)
+    score(2, 1, 0)
+    score(2, 0, 1)
+    corner(1)
+    corner(3)
+    corner(2)
+
+    group = jnp.where(member, 1.0, 0.0).astype(jnp.bfloat16)
+
+    def total(values):
+        high = values.astype(jnp.bfloat16)
+        low = (values - high.astype(jnp.float32)).astype(jnp.bfloat16)
+        dims = (((1,), (1,)), ((), ()))
+        return lax.dot_general(group, high, dims, preferred_element_type=jnp.float32) + lax.dot_general(
+            group, low, dims, preferred_element_type=jnp.float32
+        )
+
+    part_out[...] = total(best[:, width : 2 * width])
+    back = remote(part_out, part_in, c_send.at[1], c_recv.at[1], twin)
+    back.start()
+    mine = total(best[:, 0:width])
+    for copy in list(along_z.values()) + list(side.values()) + [swap]:
+        copy.wait_send()
+    back.wait()
+    out_ref[...] = mine + part_in[...]
+
+
+def fused(query_hidden, query_mask, passage_hidden, passage_ids, passage_lengths, projection):
+    qcount, qlen, depth = query_hidden.shape
+    width = qcount * qlen
+    rows = passage_hidden.shape[1]
+    passages = PASS_GRP * lax.axis_size("gallery")
+    anywhere = pl.BlockSpec(memory_space=pltpu.HBM)
+    dma = pltpu.SemaphoreType.DMA
+    bf16, f32 = jnp.bfloat16, jnp.float32
+    return pl.pallas_call(
+        fused_kernel,
+        out_shape=jax.ShapeDtypeStruct((qcount, passages), f32),
+        in_specs=[anywhere] * 6,
+        out_specs=pl.BlockSpec(memory_space=pltpu.VMEM),
+        scratch_shapes=[
+            pltpu.VMEM((width, depth), bf16),
+            pltpu.VMEM((qcount, qlen), jnp.int32),
+            pltpu.VMEM((rows, depth), bf16),
+            pltpu.VMEM((1, rows), jnp.int32),
+            pltpu.SMEM(passage_lengths.shape, jnp.int32),
+            pltpu.VMEM((depth, DIM), bf16),
+            pltpu.VMEM((ROWS, DIM), f32),
+            pltpu.VMEM((16, ROWS, DIM), bf16),
+            pltpu.VMEM((DIM, 2 * width), bf16),
+            pltpu.VMEM((passages, 2 * width), f32),
+            pltpu.VMEM((qcount, passages), f32),
+            pltpu.VMEM((qcount, passages), f32),
+            dma((6,)), dma((4,)), dma((4,)), dma((16,)), dma((16,)), dma((2,)), dma((2,)),
+        ],
+        compiler_params=pltpu.CompilerParams(
+            collective_id=0, has_side_effects=True, vmem_limit_bytes=60 * 1024 * 1024
+        ),
+    )(query_hidden.reshape(width, depth), query_mask, passage_hidden, passage_ids, passage_lengths, projection)
+
+
 def solution(mesh):
     placed = (
         P(("query", "gallery"), None, None),
@@ -84,6 +299,7 @@
         P("gallery"),
         P(),
     )
+    small = mesh.shape["query"] == PASS_GRP and mesh.shape["gallery"] == 16
     return jax.shard_map(
-        local, mesh=mesh, in_specs=placed, out_specs=P(("query", "gallery"), None), check_vma=False
+        fused if small else local, mesh=mesh, in_specs=placed, out_specs=P(("query", "gallery"), None), check_vma=False
     )

time: 77.8 us -> 30.8 us (0.40)
  blocking collectives: 47.5 us -> 0 us
  Pallas kernels: 0 us -> 29.3 us
  between operations: 13.6 us -> 0.01 us
  matrix products: 6.51 us -> 0 us
  other arithmetic: 5.26 us -> 0 us
  local copies, waits for them, and re-layouts: 4.07 us -> 1.31 us
    all_gather x3 -> x0, blocking collectives: 47.5 us -> none  [the longest x1 25.5 us: local(): lax.all_gather(passage_unit, 'gallery', axis=0, tiled=True)]
    pallas_call x0 -> x1, Pallas kernels: none -> 29.3 us  [fused(): pl.pallas_call(fused_kernel, out_shape=jax.ShapeDtypeStruct((qcount, pass...]
    dot_general x6 -> x0, matrix products: 6.51 us -> none  [the longest x4 4.52 us: one_block(): jnp.einsum('td,rd->tr', query_unit, unit_block, preferred_element_type=jn...]
    reduce_max x4 -> x0, other arithmetic: 4.39 us -> none  [one_block(): jnp.max(jnp.where(row_slot == member, similar, NEG), axis=2)]
    all_gather x3 -> x0, local copies, waits for them, and re-layouts: 2.76 us -> none  [the longest x1 1.75 us: local(): piece_units = lax.all_gather(thin_units, 'query', axis=1, tiled=True)]
    unnamed x13 -> x1, local copies, waits for them, and re-layouts: 0.28 us -> 1.31 us
  transfers between devices with their start and end apart: 1 -> 0, of which waited for: 1 -> 0; matrix products, arithmetic and copies ran while one was open for 1% -> 0% of each run, Pallas kernels for 0% -> 0%
where the time goes in v1:
time: 30.8 us; the launch traced here: 30.6 us
  Pallas kernels  29.3 us (95%)
  local copies, waits for them, and re-layouts  1.31 us (4%)
    pallas_call x1, Pallas kernels, fused(): pl.pallas_call(fused_kernel, out_shape=jax.ShapeDtypeStruct((qcount, pass...  29.3 us
    unnamed x1, local copies, waits for them, and re-layouts  1.31 us

profile of v1, /device:TPU:0, one launch (start us, length us, event | category | flops | bytes accessed | tf_op | source)
XLA Modules:
  0.0 30.6 jit_solution(607124773867431914)
XLA Ops:
  0.0 29.3 %shard_map.64 = f32[24,32]{1,0:T(8,128)} custom-call(bf16[768,768]{1,0:T(8,128)(2,1)} %bitcast.1, s32[24,32]{1,0:T(8,128)} %mask_hbm.1, bf16[1,180,768]{2,1,0:T(8,128)(2,1)} %ph_hbm.1, s32[1,180]{1,0:T(1,128)} %ids_hbm.1, s32[2]{0:T(128)} %len_hbm.1, bf16[768,128]{1,0:T(8,128)(2,1)} %proj_hbm.1), custom_call_target="tpu_custom_call" | custom-call | tf_op jit(solution)/shard_map/pallas_call | solution.py:267
  29.3 1.3 %copy.8 = f32[24,32]{1,0:T(8,128)} copy(f32[24,32]{1,0:T(8,128)} %shard_map.64) | data formatting | bytes 6144

commit v2 on v1

--- a/solution.py
+++ b/solution.py
@@ -165,13 +165,10 @@
         passage = ((((z + d) % 4) * 2 + (y + dy) % 2) * 2 + core) * 2 + (x + dx) % 2
         held = 4 * d + 2 * dx + dy
 
-        def chunk(k, carry):
-            cols = pl.ds(pl.multiple_of(k * 256, 256), 256)
+        for k in range(2 * width // 256):
+            cols = slice(k * 256, (k + 1) * 256)
             similar = jnp.dot(blocks[held], queries[:, cols], preferred_element_type=jnp.float32)
             best[pl.ds(passage, 1), cols] = jnp.max(similar, axis=0, keepdims=True)
-            return carry
-
-        lax.fori_loop(0, 2 * width // 256, chunk, 0)
 
     side[0, 0].start()
     side[0, 1].start()

time: 30.8 us -> 21.6 us (0.70)
  Pallas kernels: 29.3 us -> 20.1 us
    pallas_call x1, Pallas kernels: 29.3 us -> 20.1 us  [fused(): pl.pallas_call(fused_kernel, out_shape=jax.ShapeDtypeStruct((qcount, pass...]
where the time goes in v2:
time: 21.6 us; the launch traced here: 21.4 us
  Pallas kernels  20.1 us (93%)
  local copies, waits for them, and re-layouts  1.31 us (6%)
    pallas_call x1, Pallas kernels, fused(): pl.pallas_call(fused_kernel, out_shape=jax.ShapeDtypeStruct((qcount, pass...  20.1 us
    unnamed x1, local copies, waits for them, and re-layouts  1.31 us

profile of v2, /device:TPU:0, one launch (start us, length us, event | category | flops | bytes accessed | tf_op | source)
XLA Modules:
  0.0 21.4 jit_solution(17247767174464969830)
XLA Ops:
  0.0 20.1 %shard_map.64 = f32[24,32]{1,0:T(8,128)} custom-call(bf16[768,768]{1,0:T(8,128)(2,1)} %bitcast.1, s32[24,32]{1,0:T(8,128)} %mask_hbm.1, bf16[1,180,768]{2,1,0:T(8,128)(2,1)} %ph_hbm.1, s32[1,180]{1,0:T(1,128)} %ids_hbm.1, s32[2]{0:T(128)} %len_hbm.1, bf16[768,128]{1,0:T(8,128)(2,1)} %proj_hbm.1), custom_call_target="tpu_custom_call" | custom-call | tf_op jit(solution)/shard_map/pallas_call | solution.py:264
  20.1 1.3 %copy.8 = f32[24,32]{1,0:T(8,128)} copy(f32[24,32]{1,0:T(8,128)} %shard_map.64) | data formatting | bytes 6144

commit v3 on v2

--- a/solution.py
+++ b/solution.py
@@ -78,14 +78,13 @@
 
 
 ROWS = 192
-HALF = 96
 MESH = pl.DeviceIdType.MESH
 
 
 def fused_kernel(
     qh_hbm, mask_hbm, ph_hbm, ids_hbm, len_hbm, proj_hbm, out_ref,
     qh, mask, ph, ids, lens, proj, padded, blocks, queries, best, part_out, part_in,
-    in_sem, z_send, z_recv, n_send, n_recv, c_send, c_recv,
+    in_sem, z_send, z_recv, n_send, n_recv, q_send, q_recv, p_send, p_recv,
 ):
     x = lax.axis_index("query")
     g = lax.axis_index("gallery")
@@ -103,9 +102,10 @@
     x_near = (1 - x, g)
     y_near = (x, at(z, 1 - y, core))
     twin = (x, at(z, y, 1 - core))
+    x_twin = (1 - x, at(z, y, 1 - core))
 
     barrier = pltpu.get_barrier_semaphore()
-    for peer in (line[1], line[2], line[3], x_near, y_near, twin):
+    for peer in (line[1], line[2], line[3], x_near, y_near, twin, x_twin):
         pl.semaphore_signal(barrier, inc=1, device_id=peer, device_id_type=MESH)
 
     loads = [
@@ -134,48 +134,6 @@
     padded[pl.ds(0, rows), :] = jnp.where(column > 0.0, unit, first)
     blocks[0] = padded[...].astype(jnp.bfloat16)
 
-    pl.semaphore_wait(barrier, 6)
-
-    def remote(src, dst, send, recv, peer):
-        return pltpu.make_async_remote_copy(
-            src_ref=src, dst_ref=dst, send_sem=send, recv_sem=recv, device_id=peer, device_id_type=MESH
-        )
-
-    along_z = {
-        d: remote(blocks.at[0], blocks.at[4 * d], z_send.at[d], z_recv.at[d], line[d]) for d in (1, 2, 3)
-    }
-
-    def near(d, kind):
-        if kind == 0:
-            pair, peer = (blocks.at[4 * d], blocks.at[4 * d + 2]), x_near
-        elif kind == 1:
-            pair, peer = (blocks.at[4 * d], blocks.at[4 * d + 1]), y_near
-        elif kind == 2:
-            half = pl.ds(0, HALF)
-            pair, peer = (blocks.at[4 * d + 2, half], blocks.at[4 * d + 3, half]), y_near
-        else:
-            half = pl.ds(HALF, HALF)
-            pair, peer = (blocks.at[4 * d + 1, half], blocks.at[4 * d + 3, half]), x_near
-        k = 4 * d + kind
-        return remote(*pair, n_send.at[k], n_recv.at[k], peer)
-
-    side = {(d, kind): near(d, kind) for d in range(4) for kind in range(4)}
-
-    def score(d, dx, dy):
-        passage = ((((z + d) % 4) * 2 + (y + dy) % 2) * 2 + core) * 2 + (x + dx) % 2
-        held = 4 * d + 2 * dx + dy
-
-        for k in range(2 * width // 256):
-            cols = slice(k * 256, (k + 1) * 256)
-            similar = jnp.dot(blocks[held], queries[:, cols], preferred_element_type=jnp.float32)
-            best[pl.ds(passage, 1), cols] = jnp.max(similar, axis=0, keepdims=True)
-
-    side[0, 0].start()
-    side[0, 1].start()
-    along_z[1].start()
-    along_z[3].start()
-    along_z[2].start()
-
     loads[4].wait()
     flags = mask[...].astype(jnp.float32)
     spread = lax.broadcasted_iota(jnp.int32, (qlen, width), 1) % qlen == lax.broadcasted_iota(jnp.int32, (qlen, width), 0)
@@ -188,50 +146,65 @@
         projected = jnp.dot(qh[cols, :], proj[...], preferred_element_type=jnp.float32).T
         unit = projected * lax.rsqrt(jnp.sum(projected * projected, axis=0, keepdims=True) + EPS)
         queries[:, cols] = (unit * weight[:, cols]).astype(jnp.bfloat16)
-    own, other = pl.ds(0, width), pl.ds(width, width)
-    swap = remote(queries.at[:, own], queries.at[:, other], c_send.at[0], c_recv.at[0], twin)
+    pl.semaphore_wait(barrier, 7)
+
+    def remote(src, dst, send, recv, peer):
+        return pltpu.make_async_remote_copy(
+            src_ref=src, dst_ref=dst, send_sem=send, recv_sem=recv, device_id=peer, device_id_type=MESH
+        )
+
+    along_z = {
+        d: remote(blocks.at[0], blocks.at[2 * d], z_send.at[d], z_recv.at[d], line[d]) for d in (1, 2, 3)
+    }
+    along_y = {
+        d: remote(blocks.at[2 * d], blocks.at[2 * d + 1], n_send.at[d], n_recv.at[d], y_near) for d in range(4)
+    }
+    quarter = [pl.ds(k * width, width) for k in range(4)]
+
+    def move(k, source, target, peer):
+        return remote(queries.at[:, quarter[source]], queries.at[:, quarter[target]], q_send.at[k], q_recv.at[k], peer)
+
+    swap, across, relay = move(0, 0, 1, twin), move(1, 0, 2, x_near), move(2, 2, 3, twin)
+
+    def score(d, dy, quarters):
+        passage = at((z + d) % 4, (y + dy) % 2, core) * 2 + x
+        for k in range(quarters[0] * width // 256, (quarters[-1] + 1) * width // 256):
+            cols = slice(k * 256, (k + 1) * 256)
+            similar = jnp.dot(blocks[2 * d + dy], queries[:, cols], preferred_element_type=jnp.float32)
+            best[pl.ds(passage, 1), cols] = jnp.max(similar, axis=0, keepdims=True)
+
+    along_z[1].start()
+    along_z[3].start()
+    along_z[2].start()
+    across.start()
+    along_y[0].start()
     swap.start()
-
-    def pass_on(d):
-        side[d, 0].wait_recv()
-        side[d, 2].start()
-        side[d, 1].wait_recv()
-        side[d, 3].start()
-
-    def corner(d):
-        side[d, 2].wait_recv()
-        side[d, 3].wait_recv()
-        score(d, 1, 1)
-
-    def from_line(d):
+    score(0, 0, [0])
+    for d in (1, 3):
         along_z[d].wait_recv()
-        side[d, 0].start()
-        side[d, 1].start()
-
-    pass_on(0)
-    from_line(1)
-    from_line(3)
+        along_y[d].start()
     swap.wait_recv()
-    score(0, 0, 0)
-    score(0, 1, 0)
-    score(0, 0, 1)
-    from_line(2)
-    score(1, 0, 0)
-    score(3, 0, 0)
-    corner(0)
-    pass_on(1)
-    score(1, 1, 0)
-    score(1, 0, 1)
-    pass_on(3)
-    score(3, 1, 0)
-    score(3, 0, 1)
-    score(2, 0, 0)
-    pass_on(2)
-    score(2, 1, 0)
-    score(2, 0, 1)
-    corner(1)
-    corner(3)
-    corner(2)
+    score(0, 0, [1])
+    score(1, 0, [0, 1])
+    score(3, 0, [0, 1])
+    along_z[2].wait_recv()
+    along_y[2].start()
+    along_y[0].wait_recv()
+    score(0, 1, [0, 1])
+    across.wait_recv()
+    relay.start()
+    score(2, 0, [0, 1])
+    early = [(0, 0), (0, 1), (1, 0), (3, 0), (2, 0)]
+    for d, dy in early:
+        score(d, dy, [2])
+    along_y[1].wait_recv()
+    score(1, 1, [0, 2])
+    relay.wait_recv()
+    for d, dy in early + [(1, 1)]:
+        score(d, dy, [3])
+    for d in (3, 2):
+        along_y[d].wait_recv()
+        score(d, 1, [0, 3])
 
     group = jnp.where(member, 1.0, 0.0).astype(jnp.bfloat16)
 
@@ -243,14 +216,18 @@
             group, low, dims, preferred_element_type=jnp.float32
         )
 
-    part_out[...] = total(best[:, width : 2 * width])
-    back = remote(part_out, part_in, c_send.at[1], c_recv.at[1], twin)
-    back.start()
+    returns = []
+    for k, peer in ((3, x_twin), (2, x_near), (1, twin)):
+        part_out[k] = total(best[:, k * width : (k + 1) * width])
+        back = remote(part_out.at[k], part_in.at[k], p_send.at[k], p_recv.at[k], peer)
+        back.start()
+        returns.append(back)
     mine = total(best[:, 0:width])
-    for copy in list(along_z.values()) + list(side.values()) + [swap]:
+    for copy in list(along_z.values()) + list(along_y.values()) + [swap, across, relay]:
         copy.wait_send()
-    back.wait()
-    out_ref[...] = mine + part_in[...]
+    for back in returns:
+        back.wait()
+    out_ref[...] = (mine + part_in[1]) + (part_in[2] + part_in[3])
 
 
 def fused(query_hidden, query_mask, passage_hidden, passage_ids, passage_lengths, projection):
@@ -274,12 +251,12 @@
             pltpu.SMEM(passage_lengths.shape, jnp.int32),
             pltpu.VMEM((depth, DIM), bf16),
             pltpu.VMEM((ROWS, DIM), f32),
-            pltpu.VMEM((16, ROWS, DIM), bf16),
-            pltpu.VMEM((DIM, 2 * width), bf16),
-            pltpu.VMEM((passages, 2 * width), f32),
-            pltpu.VMEM((qcount, passages), f32),
-            pltpu.VMEM((qcount, passages), f32),
-            dma((6,)), dma((4,)), dma((4,)), dma((16,)), dma((16,)), dma((2,)), dma((2,)),
+            pltpu.VMEM((8, ROWS, DIM), bf16),
+            pltpu.VMEM((DIM, 4 * width), bf16),
+            pltpu.VMEM((passages, 4 * width), f32),
+            pltpu.VMEM((4, qcount, passages), f32),
+            pltpu.VMEM((4, qcount, passages), f32),
+            dma((6,)), dma((4,)), dma((4,)), dma((4,)), dma((4,)), dma((3,)), dma((3,)), dma((4,)), dma((4,)),
         ],
         compiler_params=pltpu.CompilerParams(
             collective_id=0, has_side_effects=True, vmem_limit_bytes=60 * 1024 * 1024

time: 21.6 us -> 21.1 us (0.977)
  Pallas kernels: 20.1 us -> 19.5 us
    pallas_call x1, Pallas kernels: 20.1 us -> 19.5 us  [fused(): pl.pallas_call(fused_kernel, out_shape=jax.ShapeDtypeStruct((qcount, pass...]
where the time goes in v3:
time: 21.1 us; the launch traced here: 20.9 us
  Pallas kernels  19.5 us (92%)
  local copies, waits for them, and re-layouts  1.31 us (6%)
    pallas_call x1, Pallas kernels, fused(): pl.pallas_call(fused_kernel, out_shape=jax.ShapeDtypeStruct((qcount, pass...  19.5 us
    unnamed x1, local copies, waits for them, and re-layouts  1.31 us

profile of v3, /device:TPU:0, one launch (start us, length us, event | category | flops | bytes accessed | tf_op | source)
XLA Modules:
  0.0 20.9 jit_solution(3210140611752235883)
XLA Ops:
  0.0 19.5 %shard_map.64 = f32[24,32]{1,0:T(8,128)} custom-call(bf16[768,768]{1,0:T(8,128)(2,1)} %bitcast.1, s32[24,32]{1,0:T(8,128)} %mask_hbm.1, bf16[1,180,768]{2,1,0:T(8,128)(2,1)} %ph_hbm.1, s32[1,180]{1,0:T(1,128)} %ids_hbm.1, s32[2]{0:T(128)} %len_hbm.1, bf16[768,128]{1,0:T(8,128)(2,1)} %proj_hbm.1), custom_call_target="tpu_custom_call" | custom-call | tf_op jit(solution)/shard_map/pallas_call | solution.py:241
  19.6 1.3 %copy.8 = f32[24,32]{1,0:T(8,128)} copy(f32[24,32]{1,0:T(8,128)} %shard_map.64) | data formatting | bytes 6144
